TPU v7x, 512 devices: a whole 4x8x8 slice. The times are simulated.
512 devices in a mesh: row: 32 (over z_lo, y, core), col: 16 (over z_hi, x).
Axes of the slice: x: 4, y: 8, z: 8 (z_hi: 4, z_lo: 2; z = z_hi * 2 + z_lo), core: 2. Of those that a mesh axis runs over, the one named last changes fastest.
Arguments:
- tokens: bfloat16 [512, 12288], P('col', 'row'), may hold values from -6 to 6
- weight: bfloat16 [12288, 24576], P('row', 'col'), may hold values from -0.0546875 to 0.0546875
- bias: float32 [24576], P('col'), may hold values from -3 to 3
- cotangent: bfloat16 [512, 24576], P('row', 'col'), may hold values from -6 to 6
Outputs:
- activated: bfloat16 [512, 24576], P('row', 'col')
- grad_tokens: bfloat16 [512, 12288], P('col', 'row')
- grad_weight: bfloat16 [12288, 24576], P('row', 'col')
- grad_bias: float32 [24576], P('col')
All inputs are finite; a program needn't handle non-finite values.
Results may differ from a plain program's by a relative error of at most 0.007.
Values may be sent and summed in bfloat16 or wider, within the bound.
A program may use at most 64 MiB of HBM per device.

v0:
```python
import jax
import jax.numpy as jnp
from jax import lax
from jax.sharding import PartitionSpec as P

coef = 0.7978845608


def body(tokens, weight, bias, cotangent):
    panel = lax.all_gather(tokens, "col", axis=0, tiled=True)
    piece = panel
    projected = lax.psum_scatter(
        jnp.dot(piece, weight, preferred_element_type=jnp.float32),
        "row",
        scatter_dimension=0,
        tiled=True,
    )
    projected = projected + bias[None, :]
    cubic = coef * (projected + 0.044715 * projected * projected * projected)
    bent = jnp.tanh(cubic)
    activated = (0.5 * projected * (1.0 + bent)).astype(jnp.bfloat16)
    deriv = 0.5 * (1.0 + bent) + 0.5 * projected * (1.0 - bent * bent) * coef * (
        1.0 + 0.134145 * projected * projected
    )
    slope = (cotangent.astype(jnp.float32) * deriv).astype(jnp.bfloat16)
    slope_panel = lax.all_gather(slope, "row", axis=0, tiled=True)
    grad_weight = lax.dot_general(
        panel, slope_panel, (((0,), (0,)), ((), ())), preferred_element_type=jnp.float32
    ).astype(jnp.bfloat16)
    piece = slope_panel
    grad_tokens = lax.psum_scatter(
        lax.dot_general(
            piece, weight, (((1,), (1,)), ((), ())), preferred_element_type=jnp.float32
        ),
        "col",
        scatter_dimension=0,
        tiled=True,
    ).astype(jnp.bfloat16)
    grad_bias = lax.psum(jnp.sum(slope.astype(jnp.float32), axis=0), "row")
    return (activated, grad_tokens, grad_weight, grad_bias)


def solution(mesh):
    in_specs = (P("col", "row"), P("row", "col"), P("col"), P("row", "col"))
    out_specs = (P("row", "col"), P("col", "row"), P("row", "col"), P("col"))
    return jax.shard_map(body, mesh=mesh, in_specs=in_specs, out_specs=out_specs, check_vma=False)
```

profile of v0, /device:TPU:1, one launch (start us, length us, event | category | flops | bytes accessed | tf_op | source)
XLA Modules:
  0.0 348.7 jit_solution(1760498176697876002)
XLA Ops:
  7.2 0.0 copy-start
  7.2 0.0 reduce-scatter.3.cloned.1.call-start
  7.2 45.6 %all_gather.6 = bf16[512,384]{1,0:T(8,128)(2,1)S(1)} all-gather(bf16[32,384]{1,0:T(8,128)(2,1)} %param.4), channel_id=1, replica_groups=mesh['row'=32,'col'=16] {'col'}, dimensions={0}, use_global_device_ids=true | all-gather | bytes 417792 | tf_op jit(solution)/shard_map/all_gather | solution.py:10
  52.9 0.0 copy-done
  52.9 2.6 fusion.9
  55.5 0.0 copy-start.1
  55.5 0.0 copy-start.2
  55.5 0.0 reduce-scatter.3.cloned.1.call-update
  55.5 0.0 all-gather.2.cloned.1.call-start
  55.6 121.9 %reduce-scatter.3.cloned.1.call-done = f32[16,1536]{1,0:T(8,128)} async-done(((f32[512,1536]{1,0:T(8,128)}), f32[16,1536]{1,0:T(8,128)}) %reduce-scatter.3.cloned.1.call-update) | async-done | bytes 98320 | tf_op jit(solution)/shard_map/reduce_scatter | solution.py:12
  177.4 0.0 copy-done.1
  177.4 0.0 copy-done.2
  177.4 1.6 convert_reduce_fusion
  179.1 0.0 all-gather.2.cloned.1.call-update
  179.1 0.0 reduce-scatter.5.cloned.1.call-start
  179.1 67.4 %all-gather.2.cloned.1.call-done = bf16[512,1536]{1,0:T(8,128)(2,1)} async-done(((bf16[16,1536]{1,0:T(8,128)(2,1)}), bf16[512,1536]{1,0:T(8,128)(2,1)}) %all-gather.2.cloned.1.call-update) | async-done | bytes 1572880 | tf_op jit(solution)/shard_map/all_gather | solution.py:26
  246.6 3.3 fusion.10
  249.9 0.0 reduce-scatter.5.cloned.1.call-update
  249.9 54.8 %psum.7 = f32[1536]{0:T(1024)} all-reduce(f32[1536]{0:T(1024)S(1)} %get-tuple-element.8), channel_id=1, replica_groups=mesh['row'=32,'col'=16] {'row'}, use_global_device_ids=true, to_apply=%region_3.0 | all-reduce | flops 1536 | bytes 12288 | tf_op jit(solution)/shard_map/psum | solution.py:39
  304.7 2.4 fusion
  307.2 1.5 copy.8
  308.6 32.1 %reduce-scatter.5.cloned.1.call-done = f32[32,384]{1,0:T(8,128)} async-done(((f32[512,384]{1,0:T(8,128)}), f32[32,384]{1,0:T(8,128)}) %reduce-scatter.5.cloned.1.call-update) | async-done | bytes 49168 | tf_op jit(solution)/shard_map/reduce_scatter | solution.py:31
  340.8 1.4 convert_element_type.24
Async XLA Ops:
  7.2 45.7 %copy-start = (bf16[384,1536]{1,0:T(8,128)(2,1)S(1)}, bf16[384,1536]{1,0:T(8,128)(2,1)}, u32[]{:S(2)}) copy-start(bf16[384,1536]{1,0:T(8,128)(2,1)} %param.5) | copy-start | bytes 3538948
  7.2 170.3 %reduce-scatter.3.cloned.1.call-start = ((), (), s32[]{:S(2)}) async-start(), calls=%async_computation.2 | async-start | bytes 3244032 | tf_op jit(solution)/shard_map/reduce_scatter | solution.py:12
  55.5 121.9 %copy-start.1 = (bf16[16,1536]{1,0:T(8,128)(2,1)S(1)}, bf16[16,1536]{1,0:T(8,128)(2,1)}, u32[]{:S(2)}) copy-start(bf16[16,1536]{1,0:T(8,128)(2,1)} %param.7) | copy-start | bytes 147460
  55.5 121.9 %copy-start.2 = (f32[1536]{0:T(1024)S(1)}, f32[1536]{0:T(1024)}, u32[]{:S(2)}) copy-start(f32[1536]{0:T(1024)} %param.6) | copy-start | bytes 18436
  55.5 191.0 %all-gather.2.cloned.1.call-start = ((), (), s32[]{:S(2)}) async-start(), calls=%async_computation.3 | async-start | bytes 1622016 | tf_op jit(solution)/shard_map/all_gather | solution.py:26
  179.1 161.7 %reduce-scatter.5.cloned.1.call-start = ((), (), s32[]{:S(2)}) async-start(), calls=%async_computation.4 | async-start | bytes 835584 | tf_op jit(solution)/shard_map/reduce_scatter | solution.py:31
Sparse Core Ops, SparseCore 0:
  55.7 121.7 reduce-scatter.2
  180.4 66.1 all-gather.1
  251.2 89.5 reduce-scatter.4
where the time goes:
time: 350 us; the launch traced here: 349 us
  waiting for transfers between devices  221 us (63%)
  blocking collectives  100 us (29%)
  between operations  13.8 us (4%)
  matrix products  8.37 us (2%)
    reduce_scatter x1, waiting for transfers between devices, body(): lax.psum_scatter(jnp.dot(piece, weight, preferred_element_type=jnp.float3...  122 us
    all_gather x1, waiting for transfers between devices, body(): slope_panel = lax.all_gather(slope, 'row', axis=0, tiled=True)  67.4 us
    psum x1, blocking collectives, body(): grad_bias = lax.psum(jnp.sum(slope.astype(jnp.float32), axis=0), 'row')  54.8 us
    all_gather x1, blocking collectives, body(): panel = lax.all_gather(tokens, 'col', axis=0, tiled=True)  45.6 us
    reduce_scatter x1, waiting for transfers between devices, body(): lax.psum_scatter(lax.dot_general(piece, weight, (((1,), (1,)), ((), ())),...  32.1 us
  transfers between devices with their start and end apart: 3, of which 3 were waited for; matrix products, arithmetic and copies ran while one was open for 1% of the time, Pallas kernels for 0%

commit v1 on v0

v1 whole, which is shorter than its diff:
```python
import jax
import jax.numpy as jnp
from jax import lax
from jax.experimental import pallas as pl
from jax.experimental.pallas import tpu as pltpu
from jax.sharding import PartitionSpec as P

MESH = pl.DeviceIdType.MESH
coef = 0.7978845608
NX, NZH, NY, NZL = 4, 4, 8, 2
R = 16
F = 384
N = 1536
AROUND_X = (0, 1, 3, 2)
AROUND_Y = (1, 7, 2, 6, 3, 5, 4)


def dot(a, b, dims):
    return lax.dot_general(a, b, (dims, ((), ())), preferred_element_type=jnp.float32)


def kernel(
    tok_h, w_h, b_h, cot_h,
    act_h, gt_h, gw_h, gb_h,
    w2, tok, tokx, cot, bias,
    pown, zsend, zrecv, ysend, yrecv, sl,
    gown, gsend, g1recv, g2send, g2recv,
    actv, gtv, gwv, gbv,
    loc, wsem, a0s, a1s, a1r, a2s, a2r, xsem, zs, zr, ys, yr, es, ezs, er, hs, g1s, g1r, g2s, g2r,
):
    row, col = lax.axis_index("row"), lax.axis_index("col")
    core, y, zl = lax.rem(row, 2), lax.rem(lax.div(row, 2), NY), lax.div(row, 2 * NY)
    x, zh = lax.rem(col, NX), lax.div(col, NX)
    other = 1 - core

    def device(zl_=zl, y_=y, core_=core, zh_=zh, x_=x):
        return {"row": zl_ * (2 * NY) + y_ * 2 + core_, "col": zh_ * NX + x_}

    started = []

    def send(src, dst, ssem, rsem, to):
        copy = pltpu.make_async_remote_copy(
            src_ref=src, dst_ref=dst, send_sem=ssem, recv_sem=rsem, device_id=to, device_id_type=MESH
        )
        copy.start()
        return copy

    def arrived(dst, sem):
        pltpu.make_async_copy(dst, dst, sem).wait()

    w_in = pltpu.make_async_copy(w_h, w2.at[core], loc.at[0])
    tok_in = pltpu.make_async_copy(tok_h.at[pl.ds(core * R, R)], tok.at[x, core, zh], loc.at[1])
    cot_in = pltpu.make_async_copy(cot_h, cot, loc.at[2])
    b_in = pltpu.make_async_copy(b_h, bias, loc.at[3])
    for copy in (tok_in, w_in, cot_in, b_in):
        copy.start()

    barrier = pltpu.get_barrier_semaphore()
    partners = [device(core_=other), device(zl_=1 - zl)]
    partners += [device(y_=lax.rem(y + d, NY)) for d in range(1, NY)]
    partners += [device(x_=lax.rem(x + d, NX)) for d in range(1, NX)]
    partners += [device(zh_=lax.rem(zh + d, NZH), core_=h) for d in range(1, NZH) for h in range(2)]
    for p in partners:
        pl.semaphore_signal(barrier, inc=1, device_id=p, device_id_type=MESH)
    pl.semaphore_wait(barrier, len(partners))

    started.append(
        send(tok_h.at[pl.ds(other * R, R)], tok.at[x, core, zh], a0s, a1r.at[zh, core], device(core_=other))
    )
    for d in (1, 3, 2):
        to = lax.rem(zh + d, NZH)
        for h in range(2):
            started.append(
                send(tok_h.at[pl.ds(h * R, R)], tok.at[x, core, zh], a1s.at[d, h], a1r.at[zh, core], device(zh_=to, core_=h))
            )
    started.append(send(w_h, w2.at[core], wsem.at[0], wsem.at[1], device(core_=other)))

    def spread(z, d):
        for e in (1, 3, 2):
            piece = tok.at[x, :, z]
            started.append(send(piece, piece, a2s.at[d, e], a2r.at[x, z], device(x_=lax.rem(x + e, NX))))

    tok_in.wait()
    arrived(tok.at[x, other, zh], a1r.at[zh, other])
    spread(zh, 0)
    for d in (1, 3, 2):
        z = lax.rem(zh + d, NZH)
        for f in range(2):
            arrived(tok.at[x, f, z], a1r.at[z, f])
        spread(z, d)
    w_in.wait()
    arrived(w2.at[other], wsem.at[1])

    for d in AROUND_X:
        g = lax.rem(x + d, NX)
        if d:
            for z in range(NZH):
                arrived(tok.at[g, :, z], a2r.at[g, z])
        p = dot(tok[g, 0].reshape(NZH * R, F), w2[0], ((1,), (0,)))
        p += dot(tok[g, 1].reshape(NZH * R, F), w2[1], ((1,), (0,)))
        p = p.reshape(NZH, R, N)
        zsend[g] = p.astype(jnp.bfloat16)
        pown[g] = p
        started.append(
            send(zsend.at[g, pl.ds(2 * (1 - zl), 2)], zrecv.at[g], zs.at[d], zr.at[g], device(zl_=1 - zl))
        )
    started.append(send(tok.at[:, other], tokx, xsem.at[0], xsem.at[1], device(core_=other)))

    def ycopy(g, j, d):
        return pltpu.make_async_remote_copy(
            src_ref=ysend.at[g, j], dst_ref=yrecv.at[y], send_sem=ys.at[d, j], recv_sem=yr.at[y],
            device_id=device(y_=j * NX + g), device_id_type=MESH,
        )

    for d in AROUND_X:
        g = lax.rem(x + d, NX)
        arrived(zrecv.at[g], zr.at[g])
        for j in range(2):
            ysend[g, j] = (pown[g, 2 * zl + j] + zrecv[g, j].astype(jnp.float32)).astype(jnp.bfloat16)

            @pl.when(j * NX + g != y)
            def _(g=g, j=j, d=d):
                ycopy(g, j, d).start()

    cot_in.wait()
    b_in.wait()
    yx, yz = lax.rem(y, NX), lax.div(y, NX)
    v = pown[yx, 2 * zl + yz] + zrecv[yx, yz].astype(jnp.float32)
    for d in AROUND_Y:
        s = lax.rem(y + d, NY)
        arrived(yrecv.at[s], yr.at[s])
        v += yrecv[s].astype(jnp.float32)

    v += bias[...].reshape(1, N)
    bent = jnp.tanh(coef * (v + 0.044715 * v * v * v))
    actv[...] = (0.5 * v * (1.0 + bent)).astype(jnp.bfloat16)
    deriv = 0.5 * (1.0 + bent) + 0.5 * v * (1.0 - bent * bent) * coef * (1.0 + 0.134145 * v * v)
    mine = 2 * zl + yz
    sl[core, yx, mine] = (cot[...].astype(jnp.float32) * deriv).astype(jnp.bfloat16)

    def slopes(zl_, y_):
        return sl.at[core, lax.rem(y_, NX), 2 * zl_ + lax.div(y_, NX)]

    own = slopes(zl, y)
    for d in AROUND_Y:
        started.append(send(own, own, es.at[d], er.at[zl, y], device(y_=lax.rem(y + d, NY))))
    started.append(send(own, own, ezs.at[0], er.at[zl, y], device(zl_=1 - zl)))
    act_out = pltpu.make_async_copy(actv, act_h, loc.at[1])
    act_out.start()
    for d in AROUND_Y:
        s = lax.rem(y + d, NY)
        piece = slopes(zl, s)
        arrived(piece, er.at[zl, s])
        started.append(send(piece, piece, ezs.at[d], er.at[zl, s], device(zl_=1 - zl)))

    def g1copy(g, d):
        return pltpu.make_async_remote_copy(
            src_ref=gsend.at[g], dst_ref=g1recv.at[x], send_sem=g1s.at[d], recv_sem=g1r.at[x],
            device_id=device(x_=g), device_id_type=MESH,
        )

    for d in (2, 1, 3, 0):
        g = lax.rem(y + d, NX)
        for j in range(2):
            s = j * NX + g
            arrived(slopes(1 - zl, s), er.at[1 - zl, s])
        a = sl[core, g].reshape(NZH * R, N)
        for f in range(2):
            p = dot(a, w2[f], ((1,), (1,))).reshape(NZH, R, F)
            gsend[g, :, f] = p.astype(jnp.bfloat16)
            gown[g, :, f] = p

        @pl.when(g != x)
        def _(g=g, d=d):
            g1copy(g, d).start()

    started.append(send(sl.at[core], sl.at[core], hs.at[0], hs.at[1], device(core_=other)))

    tiles = 3
    wide = N // tiles
    arrived(tokx, xsem.at[1])
    arrived(sl.at[other], hs.at[1])
    mine_t = tok[:, core].reshape(NX * NZH * R, F)
    other_t = tokx[...].reshape(NX * NZH * R, F)
    for t in range(tiles):
        cut = pl.ds(t * wide, wide)
        p = dot(mine_t, sl[core, :, :, :, cut].reshape(NX * NZH * R, wide), ((0,), (0,)))
        p += dot(other_t, sl[other, :, :, :, cut].reshape(NX * NZH * R, wide), ((0,), (0,)))
        gwv[:, cut] = p.astype(jnp.bfloat16)
    gw_out = pltpu.make_async_copy(gwv, gw_h, loc.at[0])
    gw_out.start()

    def add_bias(i, total):
        return total + sl[i // 16, i // 4 % 4, i % 4].astype(jnp.float32)

    total = lax.fori_loop(0, 32, add_bias, jnp.zeros((R, N), jnp.float32))
    gbv[...] = jnp.sum(total, axis=0)
    gb_out = pltpu.make_async_copy(gbv, gb_h, loc.at[2])
    gb_out.start()

    for d in (1, 3, 2):
        s = lax.rem(x + d, NX)
        arrived(g1recv.at[s], g1r.at[s])
        gown[x] += g1recv[s].astype(jnp.float32)
    g2send[...] = gown[x].astype(jnp.bfloat16)
    for d in (1, 3, 2):
        to = lax.rem(zh + d, NZH)
        for f in range(2):
            started.append(
                send(g2send.at[to, f], g2recv.at[zh, core], g2s.at[d, f], g2r.at[zh, core], device(zh_=to, core_=f))
            )
    started.append(
        send(g2send.at[zh, other], g2recv.at[zh, core], g2s.at[0, 0], g2r.at[zh, core], device(core_=other))
    )
    same = gown[x, zh, core]
    arrived(g2recv.at[zh, other], g2r.at[zh, other])
    cross = g2recv[zh, other].astype(jnp.float32)
    for d in (1, 3, 2):
        s = lax.rem(zh + d, NZH)
        arrived(g2recv.at[s, core], g2r.at[s, core])
        same += g2recv[s, core].astype(jnp.float32)
        arrived(g2recv.at[s, other], g2r.at[s, other])
        cross += g2recv[s, other].astype(jnp.float32)
    gtv[core] = same.astype(jnp.bfloat16)
    gtv[other] = cross.astype(jnp.bfloat16)
    outs = [pltpu.make_async_copy(gtv.at[h], gt_h.at[pl.ds(h * R, R)], loc.at[3 + h]) for h in range(2)]
    for copy in outs:
        copy.start()

    for copy in started:
        copy.wait_send()
    for d in range(NX):
        g = lax.rem(x + d, NX)
        for j in range(2):

            @pl.when(j * NX + g != y)
            def _(g=g, j=j, d=d):
                ycopy(g, j, d).wait_send()

        h = lax.rem(y + d, NX)

        @pl.when(h != x)
        def _(h=h, d=d):
            g1copy(h, d).wait_send()

    for copy in (act_out, gw_out, gb_out, *outs):
        copy.wait()


def body(tokens, weight, bias, cotangent):
    bf, f32 = jnp.bfloat16, jnp.float32
    vmem, dma = pltpu.VMEM, pltpu.SemaphoreType.DMA
    scratch = [
        vmem((2, F, N), bf),
        vmem((NX, 2, NZH, R, F), bf),
        vmem((NX, NZH, R, F), bf),
        vmem((R, N), bf),
        vmem((N,), f32),
        vmem((NX, NZH, R, N), f32),
        vmem((NX, NZH, R, N), bf),
        vmem((NX, 2, R, N), bf),
        vmem((NX, 2, R, N), bf),
        vmem((NY, R, N), bf),
        vmem((2, NX, NZH, R, N), bf),
        vmem((NX, NZH, 2, R, F), f32),
        vmem((NX, NZH, 2, R, F), bf),
        vmem((NX, NZH, 2, R, F), bf),
        vmem((NZH, 2, R, F), bf),
        vmem((NZH, 2, R, F), bf),
        vmem((R, N), bf),
        vmem((2, R, F), bf),
        vmem((F, N), bf),
        vmem((N,), f32),
        dma((5,)),
        dma((2,)),
        dma,
        dma((NZH, 2)),
        dma((NZH, 2)),
        dma((NZH, NX)),
        dma((NX, NZH)),
        dma((2,)),
        dma((NX,)),
        dma((NX,)),
        dma((NX, 2)),
        dma((NY,)),
        dma((NY,)),
        dma((NY,)),
        dma((NZL, NY)),
        dma((2,)),
        dma((NX,)),
        dma((NX,)),
        dma((NZH, 2)),
        dma((NZH, 2)),
    ]
    shapes = [((R, N), bf), ((2 * R, F), bf), ((F, N), bf), ((N,), f32)]
    return pl.pallas_call(
        kernel,
        out_shape=[jax.ShapeDtypeStruct(s, t) for s, t in shapes],
        in_specs=[pl.BlockSpec(memory_space=pl.ANY)] * 4,
        out_specs=[pl.BlockSpec(memory_space=pl.ANY)] * 4,
        scratch_shapes=scratch,
        compiler_params=pltpu.CompilerParams(
            collective_id=0, has_side_effects=True, vmem_limit_bytes=40 << 20
        ),
    )(tokens, weight, bias, cotangent)


def solution(mesh):
    in_specs = (P("col", "row"), P("row", "col"), P("col"), P("row", "col"))
    out_specs = (P("row", "col"), P("col", "row"), P("row", "col"), P("col"))
    return jax.shard_map(body, mesh=mesh, in_specs=in_specs, out_specs=out_specs, check_vma=False)
```

time: 350 us -> 74.8 us (0.21)
  waiting for transfers between devices: 221 us -> 0 us
  blocking collectives: 100 us -> 0 us
  Pallas kernels: 0 us -> 67.5 us
  between operations: 13.8 us -> 0.65 us
  matrix products: 8.37 us -> 0 us
  local copies, waits for them, and re-layouts: 1.47 us -> 6.34 us
    reduce_scatter x2 -> x0, waiting for transfers between devices: 154 us -> none  [the longest x1 122 us: body(): lax.psum_scatter(jnp.dot(piece, weight, preferred_element_type=jnp.float3...]
    pallas_call x0 -> x1, Pallas kernels: none -> 67.5 us  [body(): pl.pallas_call(kernel, out_shape=[jax.ShapeDtypeStruct(s, t) for s, t in...]
    all_gather x1 -> x0, waiting for transfers between devices: 67.4 us -> none  [body(): slope_panel = lax.all_gather(slope, 'row', axis=0, tiled=True)]
    psum x1 -> x0, blocking collectives: 54.8 us -> none  [body(): grad_bias = lax.psum(jnp.sum(slope.astype(jnp.float32), axis=0), 'row')]
    all_gather x1 -> x0, blocking collectives: 45.6 us -> none  [body(): panel = lax.all_gather(tokens, 'col', axis=0, tiled=True)]
    dot_general x3 -> x0, matrix products: 8.37 us -> none  [the longest x1 3.3 us: body(): lax.dot_general(piece, weight, (((1,), (1,)), ((), ())), preferred_elemen...]
    unnamed x7 -> x12, local copies, waits for them, and re-layouts: 1.47 us -> 6.34 us
  transfers between devices with their start and end apart: 3 -> 0, of which waited for: 3 -> 0; matrix products, arithmetic and copies ran while one was open for 1% -> 0% of each run, Pallas kernels for 0% -> 0%
where the time goes in v1:
time: 74.8 us; the launch traced here: 74.5 us
  Pallas kernels  67.5 us (90%)
  local copies, waits for them, and re-layouts  6.34 us (8%)
    pallas_call x1, Pallas kernels, body(): pl.pallas_call(kernel, out_shape=[jax.ShapeDtypeStruct(s, t) for s, t in...  67.5 us
    unnamed x12, local copies, waits for them, and re-layouts  6.34 us

profile of v1, /device:TPU:1, one launch (start us, length us, event | category | flops | bytes accessed | tf_op | source)
XLA Modules:
  0.0 74.5 jit_solution(6194476283204343981)
XLA Ops:
  0.6 0.0 copy-start
  0.6 1.3 %copy-done = bf16[384,1536]{1,0:T(8,128)(2,1)S(1)} copy-done((bf16[384,1536]{1,0:T(8,128)(2,1)S(1)}, bf16[384,1536]{1,0:T(8,128)(2,1)}, u32[]{:S(2)}) %copy-start) | copy-done | bytes 1179672
  1.9 0.0 copy-start.1
  1.9 0.8 %copy-done.1 = bf16[16,1536]{1,0:T(8,128)(2,1)S(1)} copy-done((bf16[16,1536]{1,0:T(8,128)(2,1)S(1)}, bf16[16,1536]{1,0:T(8,128)(2,1)}, u32[]{:S(2)}) %copy-start.1) | copy-done | bytes 49176
  2.7 0.0 copy-start.2
  2.7 0.7 copy-done.2
  3.4 0.0 copy-start.3
  3.4 0.7 copy-done.3
  4.1 67.5 %shard_map.75 = (bf16[16,1536]{1,0:T(8,128)(2,1)S(1)}, bf16[32,384]{1,0:T(8,128)(2,1)S(1)}, bf16[384,1536]{1,0:T(8,128)(2,1)S(1)}, f32[1536]{0:T(1024)S(1)}) custom-call(bf16[32,384]{1,0:T(8,128)(2,1)S(1)} %copy-done.2, bf16[384,1536]{1,0:T(8,128)(2,1)S(1)} %copy-done, f32[1536]{0:T(1024)S(1)} %copy-done.3, bf16[16,1536]{1,0:T(8,128)(2,1)S(1)} %copy-done.1), custom_call_target="tpu_custom_call" | custom-call | tf_op jit(solution)/shard_map/pallas_call | solution.py:296
  71.7 0.6 copy.12
  72.3 0.6 copy.13
  72.9 1.0 %copy.14 = bf16[384,1536]{1,0:T(8,128)(2,1)} copy(bf16[384,1536]{1,0:T(8,128)(2,1)S(1)} %get-tuple-element.10) | data formatting | bytes 2359296
  73.9 0.6 copy.15
Async XLA Ops:
  0.6 1.3 %copy-start = (bf16[384,1536]{1,0:T(8,128)(2,1)S(1)}, bf16[384,1536]{1,0:T(8,128)(2,1)}, u32[]{:S(2)}) copy-start(bf16[384,1536]{1,0:T(8,128)(2,1)} %w_h.1) | copy-start | bytes 3538948
  1.9 0.8 %copy-start.1 = (bf16[16,1536]{1,0:T(8,128)(2,1)S(1)}, bf16[16,1536]{1,0:T(8,128)(2,1)}, u32[]{:S(2)}) copy-start(bf16[16,1536]{1,0:T(8,128)(2,1)} %cot_h.1) | copy-start | bytes 147460
  2.7 0.7 copy-start.2
  3.4 0.7 copy-start.3

commit v2 on v1

--- a/solution.py
+++ b/solution.py
@@ -22,7 +22,7 @@
 def kernel(
     tok_h, w_h, b_h, cot_h,
     act_h, gt_h, gw_h, gb_h,
-    w2, tok, tokx, cot, bias,
+    w2, wt, tok, tokx, cot, bias,
     pown, zsend, zrecv, ysend, yrecv, sl,
     gown, gsend, g1recv, g2send, g2recv,
     actv, gtv, gwv, gbv,
@@ -75,24 +75,27 @@
             )
     started.append(send(w_h, w2.at[core], wsem.at[0], wsem.at[1], device(core_=other)))
 
-    def spread(z, d):
-        for e in (1, 3, 2):
+    def spread(z, d, es):
+        for e in es:
             piece = tok.at[x, :, z]
             started.append(send(piece, piece, a2s.at[d, e], a2r.at[x, z], device(x_=lax.rem(x + e, NX))))
 
     tok_in.wait()
     arrived(tok.at[x, other, zh], a1r.at[zh, other])
-    spread(zh, 0)
+    spread(zh, 0, (1, 3))
     for d in (1, 3, 2):
         z = lax.rem(zh + d, NZH)
         for f in range(2):
             arrived(tok.at[x, f, z], a1r.at[z, f])
-        spread(z, d)
+        spread(z, d, (1, 3))
     w_in.wait()
     arrived(w2.at[other], wsem.at[1])
 
     for d in AROUND_X:
         g = lax.rem(x + d, NX)
+        if d == 1:
+            for e in range(NZH):
+                spread(lax.rem(zh + e, NZH), e, (2,))
         if d:
             for z in range(NZH):
                 arrived(tok.at[g, :, z], a2r.at[g, z])
@@ -106,6 +109,9 @@
         )
     started.append(send(tok.at[:, other], tokx, xsem.at[0], xsem.at[1], device(core_=other)))
 
+    for f in range(2):
+        wt[f] = w2[f].T
+
     def ycopy(g, j, d):
         return pltpu.make_async_remote_copy(
             src_ref=ysend.at[g, j], dst_ref=yrecv.at[y], send_sem=ys.at[d, j], recv_sem=yr.at[y],
@@ -166,7 +172,7 @@
             arrived(slopes(1 - zl, s), er.at[1 - zl, s])
         a = sl[core, g].reshape(NZH * R, N)
         for f in range(2):
-            p = dot(a, w2[f], ((1,), (1,))).reshape(NZH, R, F)
+            p = dot(a, wt[f], ((1,), (0,))).reshape(NZH, R, F)
             gsend[g, :, f] = p.astype(jnp.bfloat16)
             gown[g, :, f] = p
 
@@ -247,11 +253,21 @@
         copy.wait()
 
 
+def deliver(*refs):
+    sems = refs[8]
+    copies = [pltpu.make_async_copy(refs[i], refs[4 + i], sems.at[i]) for i in range(4)]
+    for copy in copies:
+        copy.start()
+    for copy in copies:
+        copy.wait()
+
+
 def body(tokens, weight, bias, cotangent):
     bf, f32 = jnp.bfloat16, jnp.float32
     vmem, dma = pltpu.VMEM, pltpu.SemaphoreType.DMA
     scratch = [
         vmem((2, F, N), bf),
+        vmem((2, N, F), bf),
         vmem((NX, 2, NZH, R, F), bf),
         vmem((NX, NZH, R, F), bf),
         vmem((R, N), bf),
@@ -292,17 +308,25 @@
         dma((NZH, 2)),
         dma((NZH, 2)),
     ]
-    shapes = [((R, N), bf), ((2 * R, F), bf), ((F, N), bf), ((N,), f32)]
-    return pl.pallas_call(
+    results = [((R, N), bf), ((2 * R, F), bf), ((F, N), bf), ((N,), f32)]
+    shapes = [jax.ShapeDtypeStruct(s, t) for s, t in results]
+    outs = pl.pallas_call(
         kernel,
-        out_shape=[jax.ShapeDtypeStruct(s, t) for s, t in shapes],
-        in_specs=[pl.BlockSpec(memory_space=pl.ANY)] * 4,
+        out_shape=shapes,
+        in_specs=[pl.BlockSpec(memory_space=pltpu.HBM)] * 4,
         out_specs=[pl.BlockSpec(memory_space=pl.ANY)] * 4,
         scratch_shapes=scratch,
         compiler_params=pltpu.CompilerParams(
-            collective_id=0, has_side_effects=True, vmem_limit_bytes=40 << 20
+            collective_id=0, has_side_effects=True, vmem_limit_bytes=60 << 20
         ),
     )(tokens, weight, bias, cotangent)
+    return pl.pallas_call(
+        deliver,
+        out_shape=shapes,
+        in_specs=[pl.BlockSpec(memory_space=pl.ANY)] * 4,
+        out_specs=[pl.BlockSpec(memory_space=pltpu.HBM)] * 4,
+        scratch_shapes=[dma((4,))],
+    )(*outs)
 
 
 def solution(mesh):

time: 74.8 us -> 107 us (1.43)
  Pallas kernels: 67.5 us -> 106 us
  local copies, waits for them, and re-layouts: 6.34 us -> 0 us
    pallas_call x1 -> x2, Pallas kernels: 67.5 us -> 106 us  [the longest x1 66.7 us: body(): pl.pallas_call(kernel, out_shape=shapes, in_specs=[pl.BlockSpec(memory_sp...]
    unnamed x12 -> x0, local copies, waits for them, and re-layouts: 6.34 us -> none
where the time goes in v2:
time: 107 us
  Pallas kernels  106 us (99%)
    pallas_call x1, Pallas kernels, body(): pl.pallas_call(kernel, out_shape=shapes, in_specs=[pl.BlockSpec(memory_sp...  66.7 us
    pallas_call x1, Pallas kernels, body(): pl.pallas_call(deliver, out_shape=shapes, in_specs=[pl.BlockSpec(memory_s...  39.3 us

profile of v2, /device:TPU:1, one launch (start us, length us, event | category | flops | bytes accessed | tf_op | source)
XLA Modules:
  0.0 106.6 jit_solution(541486162547272770)
XLA Ops:
  0.6 66.7 %shard_map.75 = (bf16[16,1536]{1,0:T(8,128)(2,1)}, bf16[32,384]{1,0:T(8,128)(2,1)}, bf16[384,1536]{1,0:T(8,128)(2,1)}, f32[1536]{0:T(1024)}) custom-call(bf16[32,384]{1,0:T(8,128)(2,1)} %tok_h.1, bf16[384,1536]{1,0:T(8,128)(2,1)} %w_h.1, f32[1536]{0:T(1024)} %b_h.1, bf16[16,1536]{1,0:T(8,128)(2,1)} %cot_h.1), custom_call_target="tpu_custom_call" | custom-call | tf_op jit(solution)/shard_map/pallas_call | solution.py:313
  67.3 39.3 %shard_map.76 = (bf16[16,1536]{1,0:T(8,128)(2,1)}, bf16[32,384]{1,0:T(8,128)(2,1)}, bf16[384,1536]{1,0:T(8,128)(2,1)}, f32[1536]{0:T(1024)}) custom-call(bf16[16,1536]{1,0:T(8,128)(2,1)} %get-tuple-element.8.refs_0_, bf16[32,384]{1,0:T(8,128)(2,1)} %get-tuple-element.9.refs_1_, bf16[384,1536]{1,0:T(8,128)(2,1)} %get-tuple-element.10.refs_2_, ...), custom_call_target="tpu_custom_call" | custom-call | tf_op jit(solution)/shard_map/pallas_call | solution.py:323

commit v3 on v2

v3 whole, which is shorter than its diff:
```python
import jax
import jax.numpy as jnp
from jax import lax
from jax.experimental import pallas as pl
from jax.experimental.pallas import tpu as pltpu
from jax.sharding import PartitionSpec as P

MESH = pl.DeviceIdType.MESH
coef = 0.7978845608
NX, NZH, NY, NZL = 4, 4, 8, 2
R = 16
F = 384
N = 1536
HALVES = 2
W = N // HALVES
AROUND_X = (0, 1, 3, 2)
AROUND_Y = (1, 7, 2, 6, 3, 5, 4)


def dot(a, b, dims):
    return lax.dot_general(a, b, (dims, ((), ())), preferred_element_type=jnp.float32)


def kernel(
    tok_h, w_h, b_h, cot_h,
    act, gt, gw, gb,
    w2, wt, tok, tokx, cot, bias,
    pown, zsend, zrecv, ysend, yrecv, sl,
    gown, gsend, g1recv, g2send, g2recv,
    loc, wsem, a0s, a1s, a1r, a2s, a2r, xsem, zs, zr, ys, yr, es, ezs, er, hs, g1s, g1r, g2s, g2r,
):
    row, col = lax.axis_index("row"), lax.axis_index("col")
    core, y, zl = lax.rem(row, 2), lax.rem(lax.div(row, 2), NY), lax.div(row, 2 * NY)
    x, zh = lax.rem(col, NX), lax.div(col, NX)
    other = 1 - core

    def device(zl_=zl, y_=y, core_=core, zh_=zh, x_=x):
        return {"row": zl_ * (2 * NY) + y_ * 2 + core_, "col": zh_ * NX + x_}

    started = []

    def send(src, dst, ssem, rsem, to):
        copy = pltpu.make_async_remote_copy(
            src_ref=src, dst_ref=dst, send_sem=ssem, recv_sem=rsem, device_id=to, device_id_type=MESH
        )
        copy.start()
        return copy

    def arrived(dst, sem):
        pltpu.make_async_copy(dst, dst, sem).wait()

    w_in = pltpu.make_async_copy(w_h, w2.at[core], loc.at[0])
    tok_in = pltpu.make_async_copy(tok_h.at[pl.ds(core * R, R)], tok.at[x, core, zh], loc.at[1])
    cot_in = pltpu.make_async_copy(cot_h, cot, loc.at[2])
    b_in = pltpu.make_async_copy(b_h, bias, loc.at[3])
    for copy in (tok_in, w_in, cot_in, b_in):
        copy.start()

    barrier = pltpu.get_barrier_semaphore()
    partners = [device(core_=other), device(zl_=1 - zl)]
    partners += [device(y_=lax.rem(y + d, NY)) for d in range(1, NY)]
    partners += [device(x_=lax.rem(x + d, NX)) for d in range(1, NX)]
    partners += [device(zh_=lax.rem(zh + d, NZH), core_=h) for d in range(1, NZH) for h in range(2)]
    for p in partners:
        pl.semaphore_signal(barrier, inc=1, device_id=p, device_id_type=MESH)
    pl.semaphore_wait(barrier, len(partners))

    started.append(
        send(tok_h.at[pl.ds(other * R, R)], tok.at[x, core, zh], a0s, a1r.at[zh, core], device(core_=other))
    )
    for d in (1, 3, 2):
        to = lax.rem(zh + d, NZH)
        for h in range(2):
            started.append(
                send(tok_h.at[pl.ds(h * R, R)], tok.at[x, core, zh], a1s.at[d, h], a1r.at[zh, core], device(zh_=to, core_=h))
            )
    started.append(send(w_h, w2.at[core], wsem.at[0], wsem.at[1], device(core_=other)))

    def spread(z, d, es):
        for e in es:
            piece = tok.at[x, :, z]
            started.append(send(piece, piece, a2s.at[d, e], a2r.at[x, z], device(x_=lax.rem(x + e, NX))))

    tok_in.wait()
    arrived(tok.at[x, other, zh], a1r.at[zh, other])
    spread(zh, 0, (1, 3))
    for d in (1, 3, 2):
        z = lax.rem(zh + d, NZH)
        for f in range(2):
            arrived(tok.at[x, f, z], a1r.at[z, f])
        spread(z, d, (1, 3))
    w_in.wait()
    arrived(w2.at[other], wsem.at[1])

    def zcopy(h, g, d):
        return send(
            zsend.at[h, g, pl.ds(2 * (1 - zl), 2)], zrecv.at[h, g], zs.at[h, d], zr.at[h, g], device(zl_=1 - zl)
        )

    for d in AROUND_X:
        g = lax.rem(x + d, NX)
        if d == 1:
            for e in range(NZH):
                spread(lax.rem(zh + e, NZH), e, (2,))
        if d:
            for z in range(NZH):
                arrived(tok.at[g, :, z], a2r.at[g, z])
        p = dot(tok[g, 0].reshape(NZH * R, F), w2[0], ((1,), (0,)))
        p += dot(tok[g, 1].reshape(NZH * R, F), w2[1], ((1,), (0,)))
        p = p.reshape(NZH, R, N)
        for h in range(HALVES):
            q = p[:, :, h * W : (h + 1) * W]
            zsend[h, g] = q.astype(jnp.bfloat16)
            pown[h, g] = q
        started.append(zcopy(0, g, d))
        if d == 0:
            started.append(zcopy(1, g, d))
    started.append(send(tok.at[:, other], tokx, xsem.at[0], xsem.at[1], device(core_=other)))

    def ycopy(h, g, j, d):
        return pltpu.make_async_remote_copy(
            src_ref=ysend.at[h, g, j], dst_ref=yrecv.at[h, y], send_sem=ys.at[h, d, j], recv_sem=yr.at[h, y],
            device_id=device(y_=j * NX + g), device_id_type=MESH,
        )

    for h in range(HALVES):
        for d in AROUND_X:
            g = lax.rem(x + d, NX)
            arrived(zrecv.at[h, g], zr.at[h, g])
            for j in range(2):
                total = pown[h, g, 2 * zl + j] + zrecv[h, g, j].astype(jnp.float32)
                ysend[h, g, j] = total.astype(jnp.bfloat16)

                @pl.when(j * NX + g != y)
                def _(h=h, g=g, j=j, d=d):
                    ycopy(h, g, j, d).start()

            if h == 0 and d:
                started.append(zcopy(1, g, d))
    for f in range(2):
        wt[f] = w2[f].T

    def slopes(h, zl_, y_):
        return sl.at[h, core, lax.rem(y_, NX), 2 * zl_ + lax.div(y_, NX)]

    cot_in.wait()
    b_in.wait()
    yx, yz = lax.rem(y, NX), lax.div(y, NX)
    mine = 2 * zl + yz
    for h in range(HALVES):
        cut = slice(h * W, (h + 1) * W)
        v = pown[h, yx, mine] + zrecv[h, yx, yz].astype(jnp.float32)
        for d in AROUND_Y:
            s = lax.rem(y + d, NY)
            arrived(yrecv.at[h, s], yr.at[h, s])
            v += yrecv[h, s].astype(jnp.float32)

        v += bias[cut].reshape(1, W)
        bent = jnp.tanh(coef * (v + 0.044715 * v * v * v))
        act[:, cut] = (0.5 * v * (1.0 + bent)).astype(jnp.bfloat16)
        deriv = 0.5 * (1.0 + bent) + 0.5 * v * (1.0 - bent * bent) * coef * (1.0 + 0.134145 * v * v)
        sl[h, core, yx, mine] = (cot[:, cut].astype(jnp.float32) * deriv).astype(jnp.bfloat16)
        own = slopes(h, zl, y)
        for d in AROUND_Y:
            started.append(send(own, own, es.at[h, d], er.at[h, zl, y], device(y_=lax.rem(y + d, NY))))
        started.append(send(own, own, ezs.at[h, 0], er.at[h, zl, y], device(zl_=1 - zl)))
    for h in range(HALVES):
        for d in AROUND_Y:
            s = lax.rem(y + d, NY)
            piece = slopes(h, zl, s)
            arrived(piece, er.at[h, zl, s])
            started.append(send(piece, piece, ezs.at[h, d], er.at[h, zl, s], device(zl_=1 - zl)))

    def g1copy(g, d):
        return pltpu.make_async_remote_copy(
            src_ref=gsend.at[g], dst_ref=g1recv.at[x], send_sem=g1s.at[d], recv_sem=g1r.at[x],
            device_id=device(x_=g), device_id_type=MESH,
        )

    for h in range(HALVES):
        for d in (2, 1, 3, 0):
            g = lax.rem(y + d, NX)
            for j in range(2):
                s = j * NX + g
                arrived(slopes(h, 1 - zl, s), er.at[h, 1 - zl, s])
            a = sl[h, core, g].reshape(NZH * R, W)
            for f in range(2):
                p = dot(a, wt[f, h * W : (h + 1) * W], ((1,), (0,))).reshape(NZH, R, F)
                if h:
                    p += gown[g, :, f]
                gown[g, :, f] = p
                if h == HALVES - 1:
                    gsend[g, :, f] = p.astype(jnp.bfloat16)

            if h == HALVES - 1:

                @pl.when(g != x)
                def _(g=g, d=d):
                    g1copy(g, d).start()

        started.append(send(sl.at[h, core], sl.at[h, core], hs.at[0, h], hs.at[1, h], device(core_=other)))

    arrived(tokx, xsem.at[1])
    mine_t = tok[:, core].reshape(NX * NZH * R, F)
    other_t = tokx[...].reshape(NX * NZH * R, F)
    for h in range(HALVES):
        cut = slice(h * W, (h + 1) * W)
        arrived(sl.at[h, other], hs.at[1, h])
        p = dot(mine_t, sl[h, core].reshape(NX * NZH * R, W), ((0,), (0,)))
        p += dot(other_t, sl[h, other].reshape(NX * NZH * R, W), ((0,), (0,)))
        gw[:, cut] = p.astype(jnp.bfloat16)

        def add_bias(i, total, h=h):
            return total + sl[h, i // 16, i // 4 % 4, i % 4].astype(jnp.float32)

        total = lax.fori_loop(0, 32, add_bias, jnp.zeros((R, W), jnp.float32))
        gb[cut] = jnp.sum(total, axis=0)

    for d in (1, 3, 2):
        s = lax.rem(x + d, NX)
        arrived(g1recv.at[s], g1r.at[s])
        gown[x] += g1recv[s].astype(jnp.float32)
    g2send[...] = gown[x].astype(jnp.bfloat16)
    for d in (1, 3, 2):
        to = lax.rem(zh + d, NZH)
        for f in range(2):
            started.append(
                send(g2send.at[to, f], g2recv.at[zh, core], g2s.at[d, f], g2r.at[zh, core], device(zh_=to, core_=f))
            )
    started.append(
        send(g2send.at[zh, other], g2recv.at[zh, core], g2s.at[0, 0], g2r.at[zh, core], device(core_=other))
    )
    for copy in started[:-7]:
        copy.wait_send()
    for d in range(NX):
        g = lax.rem(x + d, NX)
        for h in range(HALVES):
            for j in range(2):

                @pl.when(j * NX + g != y)
                def _(h=h, g=g, j=j, d=d):
                    ycopy(h, g, j, d).wait_send()

        to = lax.rem(y + d, NX)

        @pl.when(to != x)
        def _(to=to, d=d):
            g1copy(to, d).wait_send()

    same = gown[x, zh, core]
    arrived(g2recv.at[zh, other], g2r.at[zh, other])
    cross = g2recv[zh, other].astype(jnp.float32)
    for d in (1, 3, 2):
        s = lax.rem(zh + d, NZH)
        arrived(g2recv.at[s, core], g2r.at[s, core])
        same += g2recv[s, core].astype(jnp.float32)
        arrived(g2recv.at[s, other], g2r.at[s, other])
        cross += g2recv[s, other].astype(jnp.float32)
    gt[pl.ds(pl.multiple_of(core * R, R), R)] = same.astype(jnp.bfloat16)
    gt[pl.ds(pl.multiple_of(other * R, R), R)] = cross.astype(jnp.bfloat16)
    for copy in started[-7:]:
        copy.wait_send()


def deliver(*refs):
    results, outs, held, sems = refs[:4], refs[4:8], refs[8:12], refs[12]
    into = [pltpu.make_async_copy(results[i], held[i], sems.at[0, i]) for i in range(4)]
    out = [pltpu.make_async_copy(held[i], outs[i], sems.at[1, i]) for i in range(4)]
    for copy in into:
        copy.start()
    for i in (0, 1, 3, 2):
        into[i].wait()
        out[i].start()
    for copy in out:
        copy.wait()


def body(tokens, weight, bias, cotangent):
    bf, f32 = jnp.bfloat16, jnp.float32
    vmem, dma = pltpu.VMEM, pltpu.SemaphoreType.DMA
    scratch = [
        vmem((2, F, N), bf),
        vmem((2, N, F), bf),
        vmem((NX, 2, NZH, R, F), bf),
        vmem((NX, NZH, R, F), bf),
        vmem((R, N), bf),
        vmem((N,), f32),
        vmem((HALVES, NX, NZH, R, W), f32),
        vmem((HALVES, NX, NZH, R, W), bf),
        vmem((HALVES, NX, 2, R, W), bf),
        vmem((HALVES, NX, 2, R, W), bf),
        vmem((HALVES, NY, R, W), bf),
        vmem((HALVES, 2, NX, NZH, R, W), bf),
        vmem((NX, NZH, 2, R, F), f32),
        vmem((NX, NZH, 2, R, F), bf),
        vmem((NX, NZH, 2, R, F), bf),
        vmem((NZH, 2, R, F), bf),
        vmem((NZH, 2, R, F), bf),
        dma((4,)),
        dma((2,)),
        dma,
        dma((NZH, 2)),
        dma((NZH, 2)),
        dma((NZH, NX)),
        dma((NX, NZH)),
        dma((2,)),
        dma((HALVES, NX)),
        dma((HALVES, NX)),
        dma((HALVES, NX, 2)),
        dma((HALVES, NY)),
        dma((HALVES, NY)),
        dma((HALVES, NY)),
        dma((HALVES, NZL, NY)),
        dma((2, HALVES)),
        dma((NX,)),
        dma((NX,)),
        dma((NZH, 2)),
        dma((NZH, 2)),
    ]
    results = [((R, N), bf), ((2 * R, F), bf), ((F, N), bf), ((N,), f32)]
    shapes = [jax.ShapeDtypeStruct(s, t) for s, t in results]
    outs = pl.pallas_call(
        kernel,
        out_shape=shapes,
        in_specs=[pl.BlockSpec(memory_space=pltpu.HBM)] * 4,
        out_specs=[pl.BlockSpec(memory_space=pltpu.VMEM)] * 4,
        scratch_shapes=scratch,
        compiler_params=pltpu.CompilerParams(
            collective_id=0, has_side_effects=True, vmem_limit_bytes=60 << 20
        ),
    )(tokens, weight, bias, cotangent)
    return pl.pallas_call(
        deliver,
        out_shape=shapes,
        in_specs=[pl.BlockSpec(memory_space=pl.ANY)] * 4,
        out_specs=[pl.BlockSpec(memory_space=pl.ANY)] * 4,
        scratch_shapes=[vmem(s, t) for s, t in results] + [dma((2, 4))],
        compiler_params=pltpu.CompilerParams(vmem_limit_bytes=60 << 20),
    )(*outs)


def solution(mesh):
    in_specs = (P("col", "row"), P("row", "col"), P("col"), P("row", "col"))
    out_specs = (P("row", "col"), P("col", "row"), P("row", "col"), P("col"))
    return jax.shard_map(body, mesh=mesh, in_specs=in_specs, out_specs=out_specs, check_vma=False)
```

time: 107 us -> 67.4 us (0.63)
  Pallas kernels: 106 us -> 66.6 us
    pallas_call x1, Pallas kernels: 39.3 us -> 2.4 us  [body(): pl.pallas_call(deliver, out_shape=shapes, in_specs=[pl.BlockSpec(memory_s...]
    pallas_call x1, Pallas kernels: 66.7 us -> 64.2 us  [body(): pl.pallas_call(kernel, out_shape=shapes, in_specs=[pl.BlockSpec(memory_sp...]
where the time goes in v3:
time: 67.4 us; the launch traced here: 67.2 us
  Pallas kernels  66.6 us (99%)
    pallas_call x1, Pallas kernels, body(): pl.pallas_call(kernel, out_shape=shapes, in_specs=[pl.BlockSpec(memory_sp...  64.2 us
    pallas_call x1, Pallas kernels, body(): pl.pallas_call(deliver, out_shape=shapes, in_specs=[pl.BlockSpec(memory_s...  2.4 us

profile of v3, /device:TPU:1, one launch (start us, length us, event | category | flops | bytes accessed | tf_op | source)
XLA Modules:
  0.0 67.2 jit_solution(7190436175046481399)
XLA Ops:
  0.6 64.2 %shard_map.75 = (bf16[16,1536]{1,0:T(8,128)(2,1)}, bf16[32,384]{1,0:T(8,128)(2,1)}, bf16[384,1536]{1,0:T(8,128)(2,1)}, f32[1536]{0:T(1024)}) custom-call(bf16[32,384]{1,0:T(8,128)(2,1)} %tok_h.1, bf16[384,1536]{1,0:T(8,128)(2,1)} %w_h.1, f32[1536]{0:T(1024)} %b_h.1, bf16[16,1536]{1,0:T(8,128)(2,1)} %cot_h.1), custom_call_target="tpu_custom_call" | custom-call | tf_op jit(solution)/shard_map/pallas_call | solution.py:322
  64.8 2.4 %shard_map.76 = (bf16[16,1536]{1,0:T(8,128)(2,1)}, bf16[32,384]{1,0:T(8,128)(2,1)}, bf16[384,1536]{1,0:T(8,128)(2,1)}, f32[1536]{0:T(1024)}) custom-call(bf16[16,1536]{1,0:T(8,128)(2,1)} %get-tuple-element.8.refs_0_, bf16[32,384]{1,0:T(8,128)(2,1)} %get-tuple-element.9.refs_1_, bf16[384,1536]{1,0:T(8,128)(2,1)} %get-tuple-element.10.refs_2_, ...), custom_call_target="tpu_custom_call" | custom-call | tf_op jit(solution)/shard_map/pallas_call | solution.py:332

commit v4 on v3

--- a/solution.py
+++ b/solution.py
@@ -15,6 +15,7 @@
 W = N // HALVES
 AROUND_X = (0, 1, 3, 2)
 AROUND_Y = (1, 7, 2, 6, 3, 5, 4)
+PAIRS = (2, 1, 3, 0)
 
 
 def dot(a, b, dims):
@@ -26,8 +27,8 @@
     act, gt, gw, gb,
     w2, wt, tok, tokx, cot, bias,
     pown, zsend, zrecv, ysend, yrecv, sl,
-    gown, gsend, g1recv, g2send, g2recv,
-    loc, wsem, a0s, a1s, a1r, a2s, a2r, xsem, zs, zr, ys, yr, es, ezs, er, hs, g1s, g1r, g2s, g2r,
+    gown, gsend, g1recv, g2send, g2recv, g3recv,
+    loc, wsem, a0s, a1s, a1r, a2s, a2r, a3s, a3r, xsem, zs, zr, ys, yr, es, ezs, er, hs, g1s, g1r, g2s, g2r, g3s, g3r,
 ):
     row, col = lax.axis_index("row"), lax.axis_index("col")
     core, y, zl = lax.rem(row, 2), lax.rem(lax.div(row, 2), NY), lax.div(row, 2 * NY)
@@ -59,12 +60,17 @@
     barrier = pltpu.get_barrier_semaphore()
     partners = [device(core_=other), device(zl_=1 - zl)]
     partners += [device(y_=lax.rem(y + d, NY)) for d in range(1, NY)]
-    partners += [device(x_=lax.rem(x + d, NX)) for d in range(1, NX)]
+    partners += [device(x_=lax.rem(x + d, NX), core_=h) for d in range(1, NX) for h in range(2)]
     partners += [device(zh_=lax.rem(zh + d, NZH), core_=h) for d in range(1, NZH) for h in range(2)]
     for p in partners:
         pl.semaphore_signal(barrier, inc=1, device_id=p, device_id_type=MESH)
     pl.semaphore_wait(barrier, len(partners))
 
+    def share_weight(h):
+        cut = pl.ds(h * W, W)
+        started.append(send(w_h.at[:, cut], w2.at[core, :, cut], wsem.at[0, h], wsem.at[1, h], device(core_=other)))
+
+    share_weight(0)
     started.append(
         send(tok_h.at[pl.ds(other * R, R)], tok.at[x, core, zh], a0s, a1r.at[zh, core], device(core_=other))
     )
@@ -74,7 +80,14 @@
             started.append(
                 send(tok_h.at[pl.ds(h * R, R)], tok.at[x, core, zh], a1s.at[d, h], a1r.at[zh, core], device(zh_=to, core_=h))
             )
-    started.append(send(w_h, w2.at[core], wsem.at[0], wsem.at[1], device(core_=other)))
+    for h in range(1, HALVES):
+        share_weight(h)
+    for e in (1, 3, 2):
+        to = lax.rem(x + e, NX)
+        for h in range(2):
+            started.append(
+                send(tok_h.at[pl.ds(h * R, R)], tok.at[x, core, zh], a3s.at[e, h], a3r.at[x, core], device(x_=to, core_=h))
+            )
 
     def spread(z, d, es):
         for e in es:
@@ -83,14 +96,12 @@
 
     tok_in.wait()
     arrived(tok.at[x, other, zh], a1r.at[zh, other])
-    spread(zh, 0, (1, 3))
     for d in (1, 3, 2):
         z = lax.rem(zh + d, NZH)
         for f in range(2):
             arrived(tok.at[x, f, z], a1r.at[z, f])
-        spread(z, d, (1, 3))
+        spread(z, d, (1, 3, 2))
     w_in.wait()
-    arrived(w2.at[other], wsem.at[1])
 
     def zcopy(h, g, d):
         return send(
@@ -99,22 +110,23 @@
 
     for d in AROUND_X:
         g = lax.rem(x + d, NX)
-        if d == 1:
-            for e in range(NZH):
-                spread(lax.rem(zh + e, NZH), e, (2,))
         if d:
-            for z in range(NZH):
+            for f in range(2):
+                arrived(tok.at[g, f, zh], a3r.at[g, f])
+            for e in range(1, NZH):
+                z = lax.rem(zh + e, NZH)
                 arrived(tok.at[g, :, z], a2r.at[g, z])
-        p = dot(tok[g, 0].reshape(NZH * R, F), w2[0], ((1,), (0,)))
-        p += dot(tok[g, 1].reshape(NZH * R, F), w2[1], ((1,), (0,)))
-        p = p.reshape(NZH, R, N)
         for h in range(HALVES):
-            q = p[:, :, h * W : (h + 1) * W]
-            zsend[h, g] = q.astype(jnp.bfloat16)
-            pown[h, g] = q
-        started.append(zcopy(0, g, d))
-        if d == 0:
-            started.append(zcopy(1, g, d))
+            cut = slice(h * W, (h + 1) * W)
+            if d == 0:
+                arrived(w2.at[other, :, pl.ds(h * W, W)], wsem.at[1, h])
+            p = dot(tok[g, 0].reshape(NZH * R, F), w2[0, :, cut], ((1,), (0,)))
+            p += dot(tok[g, 1].reshape(NZH * R, F), w2[1, :, cut], ((1,), (0,)))
+            p = p.reshape(NZH, R, W)
+            zsend[h, g] = p.astype(jnp.bfloat16)
+            if h == 0 or d == 0:
+                started.append(zcopy(h, g, d))
+            pown[h, g] = p
     started.append(send(tok.at[:, other], tokx, xsem.at[0], xsem.at[1], device(core_=other)))
 
     def ycopy(h, g, j, d):
@@ -135,8 +147,8 @@
                 def _(h=h, g=g, j=j, d=d):
                     ycopy(h, g, j, d).start()
 
-            if h == 0 and d:
-                started.append(zcopy(1, g, d))
+            if h < HALVES - 1 and d:
+                started.append(zcopy(h + 1, g, d))
     for f in range(2):
         wt[f] = w2[f].T
 
@@ -147,7 +159,7 @@
     b_in.wait()
     yx, yz = lax.rem(y, NX), lax.div(y, NX)
     mine = 2 * zl + yz
-    for h in range(HALVES):
+    def slope_part(h):
         cut = slice(h * W, (h + 1) * W)
         v = pown[h, yx, mine] + zrecv[h, yx, yz].astype(jnp.float32)
         for d in AROUND_Y:
@@ -160,25 +172,10 @@
         act[:, cut] = (0.5 * v * (1.0 + bent)).astype(jnp.bfloat16)
         deriv = 0.5 * (1.0 + bent) + 0.5 * v * (1.0 - bent * bent) * coef * (1.0 + 0.134145 * v * v)
         sl[h, core, yx, mine] = (cot[:, cut].astype(jnp.float32) * deriv).astype(jnp.bfloat16)
-        own = slopes(h, zl, y)
-        for d in AROUND_Y:
-            started.append(send(own, own, es.at[h, d], er.at[h, zl, y], device(y_=lax.rem(y + d, NY))))
-        started.append(send(own, own, ezs.at[h, 0], er.at[h, zl, y], device(zl_=1 - zl)))
-    for h in range(HALVES):
-        for d in AROUND_Y:
-            s = lax.rem(y + d, NY)
-            piece = slopes(h, zl, s)
-            arrived(piece, er.at[h, zl, s])
-            started.append(send(piece, piece, ezs.at[h, d], er.at[h, zl, s], device(zl_=1 - zl)))
-
-    def g1copy(g, d):
-        return pltpu.make_async_remote_copy(
-            src_ref=gsend.at[g], dst_ref=g1recv.at[x], send_sem=g1s.at[d], recv_sem=g1r.at[x],
-            device_id=device(x_=g), device_id_type=MESH,
-        )
-
-    for h in range(HALVES):
-        for d in (2, 1, 3, 0):
+        started.append(send(slopes(h, zl, y), slopes(h, zl, y), ezs.at[h, 0], er.at[h, zl, y], device(zl_=1 - zl)))
+
+    def partial(h):
+        for d in PAIRS:
             g = lax.rem(y + d, NX)
             for j in range(2):
                 s = j * NX + g
@@ -190,7 +187,9 @@
                     p += gown[g, :, f]
                 gown[g, :, f] = p
                 if h == HALVES - 1:
-                    gsend[g, :, f] = p.astype(jnp.bfloat16)
+                    q = p.astype(jnp.bfloat16)
+                    for z in range(NZH):
+                        gsend[g, lax.rem(z - zh + NZH, NZH), f] = q[z]
 
             if h == HALVES - 1:
 
@@ -198,6 +197,43 @@
                 def _(g=g, d=d):
                     g1copy(g, d).start()
 
+    def g1copy(g, d):
+        return pltpu.make_async_remote_copy(
+            src_ref=gsend.at[g, pl.ds(1, NZH - 1)], dst_ref=g1recv.at[x], send_sem=g1s.at[d], recv_sem=g1r.at[x],
+            device_id=device(x_=g), device_id_type=MESH,
+        )
+
+    def g3copy(g, d, f):
+        return pltpu.make_async_remote_copy(
+            src_ref=gsend.at[g, 0, f], dst_ref=g3recv.at[x, core], send_sem=g3s.at[d, f], recv_sem=g3r.at[x, core],
+            device_id=device(x_=g, core_=f), device_id_type=MESH,
+        )
+
+    for h in range(HALVES):
+        slope_part(h)
+        own = slopes(h, zl, y)
+        for d in AROUND_Y:
+            started.append(send(own, own, es.at[h, d], er.at[h, zl, y], device(y_=lax.rem(y + d, NY))))
+    for h in range(HALVES):
+        for d in AROUND_Y:
+            s = lax.rem(y + d, NY)
+            piece = slopes(h, zl, s)
+            arrived(piece, er.at[h, zl, s])
+            started.append(send(piece, piece, ezs.at[h, d], er.at[h, zl, s], device(zl_=1 - zl)))
+    for h in range(HALVES):
+        partial(h)
+        if h == HALVES - 1:
+            for d in PAIRS:
+                g = lax.rem(y + d, NX)
+
+                @pl.when(g != x)
+                def _(g=g, d=d):
+                    for f in range(2):
+                        g3copy(g, d, f).start()
+
+            started.append(
+                send(gsend.at[x, 0, other], g2recv.at[zh, core], g2s.at[0, 0], g2r.at[zh, core], device(core_=other))
+            )
         started.append(send(sl.at[h, core], sl.at[h, core], hs.at[0, h], hs.at[1, h], device(core_=other)))
 
     arrived(tokx, xsem.at[1])
@@ -219,18 +255,18 @@
     for d in (1, 3, 2):
         s = lax.rem(x + d, NX)
         arrived(g1recv.at[s], g1r.at[s])
-        gown[x] += g1recv[s].astype(jnp.float32)
-    g2send[...] = gown[x].astype(jnp.bfloat16)
-    for d in (1, 3, 2):
+    final = []
+    for d in (2, 1, 3):
         to = lax.rem(zh + d, NZH)
+        total = gown[x, to]
+        for e in (1, 3, 2):
+            total += g1recv[lax.rem(x + e, NX), d - 1].astype(jnp.float32)
+        g2send[d] = total.astype(jnp.bfloat16)
         for f in range(2):
-            started.append(
-                send(g2send.at[to, f], g2recv.at[zh, core], g2s.at[d, f], g2r.at[zh, core], device(zh_=to, core_=f))
+            final.append(
+                send(g2send.at[d, f], g2recv.at[zh, core], g2s.at[d, f], g2r.at[zh, core], device(zh_=to, core_=f))
             )
-    started.append(
-        send(g2send.at[zh, other], g2recv.at[zh, core], g2s.at[0, 0], g2r.at[zh, core], device(core_=other))
-    )
-    for copy in started[:-7]:
+    for copy in started:
         copy.wait_send()
     for d in range(NX):
         g = lax.rem(x + d, NX)
@@ -246,10 +282,18 @@
         @pl.when(to != x)
         def _(to=to, d=d):
             g1copy(to, d).wait_send()
+            for f in range(2):
+                g3copy(to, d, f).wait_send()
 
     same = gown[x, zh, core]
     arrived(g2recv.at[zh, other], g2r.at[zh, other])
     cross = g2recv[zh, other].astype(jnp.float32)
+    for d in (1, 3, 2):
+        s = lax.rem(x + d, NX)
+        arrived(g3recv.at[s, core], g3r.at[s, core])
+        same += g3recv[s, core].astype(jnp.float32)
+        arrived(g3recv.at[s, other], g3r.at[s, other])
+        cross += g3recv[s, other].astype(jnp.float32)
     for d in (1, 3, 2):
         s = lax.rem(zh + d, NZH)
         arrived(g2recv.at[s, core], g2r.at[s, core])
@@ -258,21 +302,8 @@
         cross += g2recv[s, other].astype(jnp.float32)
     gt[pl.ds(pl.multiple_of(core * R, R), R)] = same.astype(jnp.bfloat16)
     gt[pl.ds(pl.multiple_of(other * R, R), R)] = cross.astype(jnp.bfloat16)
-    for copy in started[-7:]:
+    for copy in final:
         copy.wait_send()
-
-
-def deliver(*refs):
-    results, outs, held, sems = refs[:4], refs[4:8], refs[8:12], refs[12]
-    into = [pltpu.make_async_copy(results[i], held[i], sems.at[0, i]) for i in range(4)]
-    out = [pltpu.make_async_copy(held[i], outs[i], sems.at[1, i]) for i in range(4)]
-    for copy in into:
-        copy.start()
-    for i in (0, 1, 3, 2):
-        into[i].wait()
-        out[i].start()
-    for copy in out:
-        copy.wait()
 
 
 def body(tokens, weight, bias, cotangent):
@@ -293,16 +324,19 @@
         vmem((HALVES, 2, NX, NZH, R, W), bf),
         vmem((NX, NZH, 2, R, F), f32),
         vmem((NX, NZH, 2, R, F), bf),
-        vmem((NX, NZH, 2, R, F), bf),
+        vmem((NX, NZH - 1, 2, R, F), bf),
         vmem((NZH, 2, R, F), bf),
         vmem((NZH, 2, R, F), bf),
+        vmem((NX, 2, R, F), bf),
         dma((4,)),
-        dma((2,)),
+        dma((2, HALVES)),
         dma,
         dma((NZH, 2)),
         dma((NZH, 2)),
         dma((NZH, NX)),
         dma((NX, NZH)),
+        dma((NX, 2)),
+        dma((NX, 2)),
         dma((2,)),
         dma((HALVES, NX)),
         dma((HALVES, NX)),
@@ -316,27 +350,21 @@
         dma((NX,)),
         dma((NZH, 2)),
         dma((NZH, 2)),
+        dma((NX, 2)),
+        dma((NX, 2)),
     ]
     results = [((R, N), bf), ((2 * R, F), bf), ((F, N), bf), ((N,), f32)]
     shapes = [jax.ShapeDtypeStruct(s, t) for s, t in results]
     outs = pl.pallas_call(
         kernel,
-        out_shape=shapes,
+        out_shape=[pltpu.VMEM(s, t) for s, t in results],
         in_specs=[pl.BlockSpec(memory_space=pltpu.HBM)] * 4,
-        out_specs=[pl.BlockSpec(memory_space=pltpu.VMEM)] * 4,
         scratch_shapes=scratch,
         compiler_params=pltpu.CompilerParams(
-            collective_id=0, has_side_effects=True, vmem_limit_bytes=60 << 20
+            collective_id=0, has_side_effects=True, vmem_limit_bytes=58 << 20
         ),
     )(tokens, weight, bias, cotangent)
-    return pl.pallas_call(
-        deliver,
-        out_shape=shapes,
-        in_specs=[pl.BlockSpec(memory_space=pl.ANY)] * 4,
-        out_specs=[pl.BlockSpec(memory_space=pl.ANY)] * 4,
-        scratch_shapes=[vmem(s, t) for s, t in results] + [dma((2, 4))],
-        compiler_params=pltpu.CompilerParams(vmem_limit_bytes=60 << 20),
-    )(*outs)
+    return outs
 
 
 def solution(mesh):

time: 67.4 us -> 66 us (0.979)
  Pallas kernels: 66.6 us -> 62.4 us
  local copies, waits for them, and re-layouts: 0 us -> 2.84 us
    pallas_call x2 -> x1, Pallas kernels: 66.6 us -> 62.4 us  [body(): pl.pallas_call(kernel, out_shape=[pltpu.VMEM(s, t) for s, t in results],...]
    unnamed x0 -> x4, local copies, waits for them, and re-layouts: none -> 2.84 us
where the time goes in v4:
time: 66 us; the launch traced here: 65.9 us
  Pallas kernels  62.4 us (95%)
  local copies, waits for them, and re-layouts  2.84 us (4%)
    pallas_call x1, Pallas kernels, body(): pl.pallas_call(kernel, out_shape=[pltpu.VMEM(s, t) for s, t in results],...  62.4 us
    unnamed x4, local copies, waits for them, and re-layouts  2.84 us

profile of v4, /device:TPU:1, one launch (start us, length us, event | category | flops | bytes accessed | tf_op | source)
XLA Modules:
  0.0 65.9 jit_solution(13804477577922528491)
XLA Ops:
  0.6 62.4 %shard_map.75 = (bf16[16,1536]{1,0:T(8,128)(2,1)S(1)}, bf16[32,384]{1,0:T(8,128)(2,1)S(1)}, bf16[384,1536]{1,0:T(8,128)(2,1)S(1)}, f32[1536]{0:T(1024)S(1)}) custom-call(bf16[32,384]{1,0:T(8,128)(2,1)} %tok_h.1, bf16[384,1536]{1,0:T(8,128)(2,1)} %w_h.1, f32[1536]{0:T(1024)} %b_h.1, bf16[16,1536]{1,0:T(8,128)(2,1)} %cot_h.1), custom_call_target="tpu_custom_call" | custom-call | tf_op jit(solution)/shard_map/pallas_call | solution.py:358
  63.0 0.6 copy.12
  63.7 0.6 copy.15
  64.3 0.6 copy.13
  64.9 1.0 %copy.14 = bf16[384,1536]{1,0:T(8,128)(2,1)} copy(bf16[384,1536]{1,0:T(8,128)(2,1)S(1)} %get-tuple-element.6) | data formatting | bytes 2359296

commit v5 on v4

--- a/solution.py
+++ b/solution.py
@@ -127,6 +127,9 @@
             if h == 0 or d == 0:
                 started.append(zcopy(h, g, d))
             pown[h, g] = p
+        if d == 0:
+            for f in range(2):
+                wt[f] = w2[f].T
     started.append(send(tok.at[:, other], tokx, xsem.at[0], xsem.at[1], device(core_=other)))
 
     def ycopy(h, g, j, d):
@@ -149,9 +152,6 @@
 
             if h < HALVES - 1 and d:
                 started.append(zcopy(h + 1, g, d))
-    for f in range(2):
-        wt[f] = w2[f].T
-
     def slopes(h, zl_, y_):
         return sl.at[h, core, lax.rem(y_, NX), 2 * zl_ + lax.div(y_, NX)]
 

time: 66 us -> 66 us (level)
  no operation moved by 1% of the time
where the time goes in v5:
time: 66 us; the launch traced here: 65.9 us
  Pallas kernels  62.4 us (95%)
  local copies, waits for them, and re-layouts  2.84 us (4%)
    pallas_call x1, Pallas kernels, body(): pl.pallas_call(kernel, out_shape=[pltpu.VMEM(s, t) for s, t in results],...  62.4 us
    unnamed x4, local copies, waits for them, and re-layouts  2.84 us

profile of v5, /device:TPU:1, one launch (start us, length us, event | category | flops | bytes accessed | tf_op | source)
XLA Modules:
  0.0 65.9 jit_solution(3219591357113702522)
XLA Ops:
  0.6 62.4 %shard_map.75 = (bf16[16,1536]{1,0:T(8,128)(2,1)S(1)}, bf16[32,384]{1,0:T(8,128)(2,1)S(1)}, bf16[384,1536]{1,0:T(8,128)(2,1)S(1)}, f32[1536]{0:T(1024)S(1)}) custom-call(bf16[32,384]{1,0:T(8,128)(2,1)} %tok_h.1, bf16[384,1536]{1,0:T(8,128)(2,1)} %w_h.1, f32[1536]{0:T(1024)} %b_h.1, bf16[16,1536]{1,0:T(8,128)(2,1)} %cot_h.1), custom_call_target="tpu_custom_call" | custom-call | tf_op jit(solution)/shard_map/pallas_call | solution.py:358
  63.0 0.6 copy.12
  63.7 0.6 copy.15
  64.3 0.6 copy.13
  64.9 1.0 %copy.14 = bf16[384,1536]{1,0:T(8,128)(2,1)} copy(bf16[384,1536]{1,0:T(8,128)(2,1)S(1)} %get-tuple-element.6) | data formatting | bytes 2359296
